TPU v7x, 256 devices: a whole 4x4x8 slice. The times are simulated.
256 devices in a mesh: ta: 4 (over x), ha: 8 (over z), wa: 8 (over y, core).
Axes of the slice: x: 4, y: 4, z: 8, core: 2. Of those that a mesh axis runs over, the one named last changes fastest.
Arguments:
- latents: float32 [8, 32, 32, 384], P('ta', 'ha', 'wa'), may hold values from -6 to 6
- first_gain: float32 [384], replicated, may hold values from 0.1 to 1.9
- first_kernel: float32 [384, 3, 3, 3, 384], P('wa'), may hold values from -0.0625 to 0.0625
- first_bias: float32 [384], replicated, may hold values from -3 to 3
- second_gain: float32 [384], replicated, may hold values from 0.1 to 1.9
- second_kernel: float32 [384, 3, 3, 3, 384], P('wa'), may hold values from -0.0625 to 0.0625
- second_bias: float32 [384], replicated, may hold values from -3 to 3
- attn_gain: float32 [384], replicated, may hold values from 0.1 to 1.9
- w_query: float32 [384, 384], replicated, may hold values from -2 to 2, as said below
- w_key: float32 [384, 384], replicated, may hold values from -2 to 2, as said below
- w_value: float32 [384, 384], replicated, may hold values from -0.3125 to 0.3125
- w_out: float32 [384, 384], replicated, may hold values from -0.3125 to 0.3125
- out_bias: float32 [384], replicated, may hold values from -3 to 3
Outputs:
- decoded: float32 [8, 32, 32, 384], P('ta', 'ha', 'wa')
Inputs may be any that keep to these rules, and one draw needn't show every extreme that they name: `w_query`: a dense matrix. `w_key`: a dense matrix.
All inputs are finite; a program needn't handle non-finite values.
Results may differ from a plain program's by a relative error of at most 0.00017.
Values sent between devices are 32-bit elements; how exact they have to be, the bound alone decides.
No kernel may reach another device: no remote copies, remote signals or barrier semaphores. Data moves between devices by JAX's collectives and lax.ppermute only.
A program may use at most 64 MiB of HBM per device.

v0:
```python
import math
import jax
import jax.numpy as jnp
from jax import lax
from jax.sharding import PartitionSpec as P


def from_behind(shard, axis, by):
    peers = lax.axis_size(axis)
    pairs = [(i, i + by) for i in range(peers) if 0 <= i + by < peers]
    return lax.ppermute(shard, axis, pairs)


def padded_2(cells, sides, width):
    for axis, dim in sides:
        count = lax.axis_size(axis)
        ends = count - 1
        head = lax.slice_in_dim(cells, 0, width, axis=dim)
        tail = lax.slice_in_dim(cells, cells.shape[dim] - width, cells.shape[dim], axis=dim)
        cells = jnp.concatenate(
            [
                lax.ppermute(tail, axis, [(i, (i + 1) % count) for i in range(ends)]),
                cells,
                lax.ppermute(head, axis, [((i + 1) % count, i) for i in range(ends)]),
            ],
            axis=dim,
        )
    return cells


def channel_norm(values, gain):
    return values * lax.rsqrt(jnp.mean(values * values, axis=-1, keepdims=True) + 1e-06) * gain


def causal_conv(activated, kernel, bias):
    frames = activated.shape[0]
    channels = activated.shape[3]
    out_count = kernel.shape[0]
    widened = lax.all_gather(activated, "wa", axis=2, tiled=True)
    earlier = from_behind(widened, "ta", 1)
    extended = jnp.concatenate([earlier, widened], axis=0)
    padded = padded_2(extended, (("ha", 1),), 1)
    padded = jnp.pad(padded, ((0, 0), (0, 0), (1, 1), (0, 0)))
    heights = activated.shape[1]
    widths = padded.shape[2] - 2
    row_count = frames * heights * widths
    summed = jnp.zeros((row_count, out_count), jnp.float32)
    for time_tap in range(3):
        patches = jnp.concatenate(
            [
                padded[
                    time_tap : time_tap + frames,
                    row_tap : row_tap + heights,
                    col_tap : col_tap + widths,
                ].reshape(row_count, channels)
                for row_tap in range(3)
                for col_tap in range(3)
            ],
            axis=1,
        )
        tap_kernel = kernel[:, time_tap].reshape(out_count, 9 * channels)
        summed = summed + lax.dot_general(
            patches,
            tap_kernel,
            (((1,), (1,)), ((), ())),
            precision=lax.Precision.HIGHEST,
            preferred_element_type=jnp.float32,
        )
    strip = summed.reshape(frames, heights, widths, out_count)
    owned = lax.all_to_all(strip, "wa", split_axis=2, concat_axis=3, tiled=True)
    return owned + bias


def absorb_keys(carry, queries, key_piece, value_piece, scale):
    top, denom, accum = carry
    scores = jnp.einsum("fqc,fkc->fqk", queries, key_piece, precision=lax.Precision.HIGHEST) * scale
    new_top = jnp.maximum(top, jnp.max(scores, axis=-1))
    weights = jnp.exp(scores - new_top[..., None])
    denom = jnp.sum(weights, axis=-1)
    accum = jnp.einsum("fqk,fkc->fqc", weights, value_piece, precision=lax.Precision.HIGHEST)
    return (new_top, denom, accum)


def per_device(
    latents,
    first_gain,
    first_kernel,
    first_bias,
    second_gain,
    second_kernel,
    second_bias,
    attn_gain,
    w_query,
    w_key,
    w_value,
    w_out,
    out_bias,
):
    inner = causal_conv(jax.nn.silu(channel_norm(latents, first_gain)), first_kernel, first_bias)
    blocked = latents + causal_conv(
        jax.nn.silu(channel_norm(inner, second_gain)), second_kernel, second_bias
    )
    frames, heights, widths, channels = blocked.shape
    cell_count = heights * widths
    normed_rows = channel_norm(blocked, attn_gain).reshape(frames * cell_count, channels)
    queries = jnp.dot(
        normed_rows, w_query, precision=lax.Precision.HIGHEST, preferred_element_type=jnp.float32
    ).reshape(frames, cell_count, channels)
    scale = 1.0 / math.sqrt(channels)
    start_state = (
        jnp.full((frames, cell_count), -1e30, jnp.float32),
        jnp.zeros((frames, cell_count), jnp.float32),
        jnp.zeros((frames, cell_count, channels), jnp.float32),
    )
    keys = jnp.dot(
        normed_rows, w_key, precision=lax.Precision.HIGHEST, preferred_element_type=jnp.float32
    ).reshape(frames, cell_count, channels)
    values = jnp.dot(
        normed_rows, w_value, precision=lax.Precision.HIGHEST, preferred_element_type=jnp.float32
    ).reshape(frames, cell_count, channels)
    top, denom, accum = absorb_keys(
        start_state,
        queries,
        lax.all_gather(keys, ("ha", "wa"), axis=1, tiled=True),
        lax.all_gather(values, ("ha", "wa"), axis=1, tiled=True),
        scale,
    )
    mixed = accum / denom[..., None]
    projected = (
        jnp.dot(
            mixed.reshape(frames * cell_count, channels),
            w_out,
            precision=lax.Precision.HIGHEST,
            preferred_element_type=jnp.float32,
        )
        + out_bias
    )
    return blocked + projected.reshape(frames, heights, widths, channels)


def solution(mesh):
    in_specs = (
        P("ta", "ha", "wa", None),
        P(),
        P("wa", None, None, None, None),
        P(),
        P(),
        P("wa", None, None, None, None),
        P(),
        P(),
        P(),
        P(),
        P(),
        P(),
        P(),
    )
    out_specs = P("ta", "ha", "wa", None)
    return jax.shard_map(
        per_device, mesh=mesh, in_specs=in_specs, out_specs=out_specs, check_vma=False
    )
```

profile of v0, /device:TPU:1, one launch (start us, length us, event | category | flops | bytes accessed | tf_op | source)
XLA Modules:
  0.0 315.1 jit_solution(18345777338632848029)
XLA Ops:
  8.5 16.1 %all_gather.12 = f32[2,4,32,384]{3,1,0,2:T(4,128)S(1)} all-gather(f32[2,4,4,384]{3,1,0,2:T(4,128)S(1)} %copy.50), channel_id=1, replica_groups=mesh['ta'=4,'ha'=8,'wa'=8] {'wa'}, dimensions={2}, use_global_device_ids=true | all-gather | bytes 442368 | tf_op jit(solution)/shard_map/all_gather | solution.py:39
  24.7 1.9 collective-permute-start
  26.6 8.3 %collective-permute-done = f32[2,4,32,384]{3,2,1,0:T(8,128)S(1)} collective-permute-done((f32[2,4,32,384]{3,2,1,0:T(8,128)S(1)}, f32[2,4,32,384]{3,2,1,0:T(8,128)S(1)}, u32[]{:S(2)}, u32[]{:S(2)}) %collective-permute-start) | collective-permute-done | bytes 393248 | tf_op jit(solution)/shard_map/ppermute | solution.py:11
  35.8 3.5 %collective-permute-start.1 = (f32[4,1,32,384]{3,2,1,0:T(8,128)}, f32[4,1,32,384]{3,2,1,0:T(8,128)S(1)}, u32[]{:S(2)}, u32[]{:S(2)}) collective-permute-start(f32[4,1,32,384]{3,2,1,0:T(8,128)} %get-tuple-element.71), channel_id=1, source_target_pairs={{0,8},{8,16},{16,24},{24,32},{32,40},{40,48},{48,56},{1,9},{9,17},... | collective-permute-start | bytes 589832 | tf_op jit(solution)/shard_map/ppermute | solution.py:22
  39.4 1.3 collective-permute-start.2
  42.6 1.4 copy.53
  44.1 1.2 reshape_squeeze.18
  45.3 1.4 copy.56
  50.0 1.4 pad_maximum_fusion.2
  52.2 3.1 fusion.24
  55.4 3.1 convolution_add_fusion.4
  58.6 3.1 convolution_add_fusion.3
  62.7 5.0 %all-to-all-start = ((f32[8,1,1536]{2,1,0:T(1,128)}), f32[8,1,1536]{2,1,0:T(1,128)S(1)}, u32[]{:S(2)}, u32[]{:S(2)}) async-start(f32[8,1,1536]{2,1,0:T(1,128)} %reshape.280), calls=%async_computation | async-start | bytes 98304 | tf_op jit(solution)/shard_map/all_to_all | solution.py:70
  67.8 4.7 %all-to-all-done = f32[8,1,1536]{2,1,0:T(1,128)S(1)} async-done(((f32[8,1,1536]{2,1,0:T(1,128)}), f32[8,1,1536]{2,1,0:T(1,128)S(1)}, u32[]{:S(2)}, u32[]{:S(2)}) %all-to-all-start) | async-done | bytes 49184 | tf_op jit(solution)/shard_map/all_to_all | solution.py:70
  74.4 13.6 %all_gather.13 = f32[2,4,32,384]{3,1,0,2:T(4,128)S(1)} all-gather(f32[2,4,4,384]{3,1,0,2:T(4,128)S(1)} %copy.61), channel_id=1, replica_groups=mesh['ta'=4,'ha'=8,'wa'=8] {'wa'}, dimensions={2}, use_global_device_ids=true | all-gather | bytes 442368 | tf_op jit(solution)/shard_map/all_gather | solution.py:39
  88.1 4.1 %collective-permute-start.3 = (f32[2,4,32,384]{3,2,1,0:T(8,128)S(1)}, f32[2,4,32,384]{3,2,1,0:T(8,128)S(1)}, u32[]{:S(2)}, u32[]{:S(2)}) collective-permute-start(f32[2,4,32,384]{3,2,1,0:T(8,128)S(1)} %copy.62), channel_id=1, source_target_pairs={{0,64},{64,128},{128,192},{1,65},{65,129},{129,193},{2,66},{66,130... | collective-permute-start | bytes 1179656 | tf_op jit(solution)/shard_map/ppermute | solution.py:11
  92.2 8.3 %collective-permute-done.3 = f32[2,4,32,384]{3,2,1,0:T(8,128)S(1)} collective-permute-done((f32[2,4,32,384]{3,2,1,0:T(8,128)S(1)}, f32[2,4,32,384]{3,2,1,0:T(8,128)S(1)}, u32[]{:S(2)}, u32[]{:S(2)}) %collective-permute-start.3) | collective-permute-done | bytes 393248 | tf_op jit(solution)/shard_map/ppermute | solution.py:11
  101.4 4.3 %collective-permute-start.4 = (f32[4,1,32,384]{3,2,1,0:T(8,128)}, f32[4,1,32,384]{3,2,1,0:T(8,128)S(1)}, u32[]{:S(2)}, u32[]{:S(2)}) collective-permute-start(f32[4,1,32,384]{3,2,1,0:T(8,128)} %get-tuple-element.65), channel_id=1, source_target_pairs={{0,8},{8,16},{16,24},{24,32},{32,40},{40,48},{48,56},{1,9},{9,17},... | collective-permute-start | bytes 589832 | tf_op jit(solution)/shard_map/ppermute | solution.py:22
  105.7 1.3 collective-permute-start.5
  107.0 2.7 fusion.17
  110.4 1.4 copy.64
  111.9 1.2 reshape_squeeze.21
  113.1 1.4 copy.67
  117.8 1.4 pad_maximum_fusion
  120.1 3.1 fusion.25
  123.2 3.1 convolution_add_fusion.2
  126.4 3.1 convolution_add_fusion.1
  130.0 8.6 %all_to_all.36 = f32[8,1,1536]{2,1,0:T(1,128)S(1)} all-to-all(f32[8,1,1536]{2,1,0:T(1,128)S(1)} %reshape.282), channel_id=1, replica_groups=mesh['ta'=4,'ha'=8,'wa'=8] {'wa'}, dimensions={0} | all-to-all | bytes 98304 | tf_op jit(solution)/shard_map/all_to_all | solution.py:70
  142.6 82.5 %all-gather.3.cloned.1.call-done = f32[2,1024,384]{2,1,0:T(8,128)} async-done(((f32[2,16,384]{2,1,0:T(8,128)}), f32[2,1024,384]{2,1,0:T(8,128)}) %all-gather.3.cloned.1.call-update) | async-done | bytes 3145744 | tf_op jit(solution)/shard_map/all_gather | solution.py:124
  225.1 4.6 %fusion.23 = (f32[2,16]{1,0:T(2,128)S(1)}, f32[2,16,1024]{2,1,0:T(8,128)S(1)}) fusion(f32[2,16,384]{2,1,0:T(8,128)S(1)} %fusion.5, f32[2,1024,384]{2,1,0:T(8,128)} %all-gather.3.cloned.1.call-done), kind=kOutput, calls=%fused_computation.126 | convolution fusion | flops 151060448 | bytes 3326080 | tf_op jit(solution)/shard_map/fqc,fkc->fqk/dot_general | solution.py:76
  229.9 73.7 %all-gather.5.cloned.1.call-done = f32[2,1024,384]{2,1,0:T(8,128)} async-done(((f32[2,16,384]{2,1,0:T(8,128)}), f32[2,1024,384]{2,1,0:T(8,128)}) %all-gather.5.cloned.1.call-update) | async-done | bytes 3145744 | tf_op jit(solution)/shard_map/all_gather | solution.py:125
  303.6 3.5 %convolution_divide_fusion = f32[2,16,384]{2,1,0:T(8,128)S(1)} fusion(f32[2,1024,384]{2,1,0:T(8,128)} %all-gather.5.cloned.1.call-done, f32[2,16,1024]{2,1,0:T(8,128)S(1)} %get-tuple-element.74, f32[2,16]{1,0:T(2,128)S(1)} %broadcast_maximum_fusion, f32[2,16]{1,0:T(2,128)S(1)} %fusion.15), kind=kOutput, calls=%fused_computation.17 | convolution fusion | flops 151040000 | bytes 3326208 | tf_op jit(solution)/shard_map/fqk,fkc->fqc/dot_general | solution.py:80
  (157 shorter events, 22.8 us)
Async XLA Ops:
  6.5 133.4 %copy-start = (f32[384,384]{1,0:T(8,128)S(1)}, f32[384,384]{1,0:T(8,128)}, u32[]{:S(2)}) copy-start(f32[384,384]{1,0:T(8,128)} %param.22) | copy-start | bytes 1769476
  6.5 34.1 %copy-start.5 = (f32[48,3,3,3,384]{4,0,3,2,1:T(8,128)S(1)}, f32[48,3,3,3,384]{4,0,3,2,1:T(8,128)}, u32[]{:S(2)}) copy-start(f32[48,3,3,3,384]{4,0,3,2,1:T(8,128)} %param.15) | copy-start | bytes 5971972
  24.7 14.7 %copy-start.6 = (f32[2,4,32,384]{3,2,1,0:T(8,128)}, f32[2,4,32,384]{3,2,1,0:T(8,128)S(1)}, u32[]{:S(2)}) copy-start(f32[2,4,32,384]{3,2,1,0:T(8,128)S(1)} %copy.51) | copy-start | bytes 1179652
  24.7 10.3 %collective-permute-start = (f32[2,4,32,384]{3,2,1,0:T(8,128)S(1)}, f32[2,4,32,384]{3,2,1,0:T(8,128)S(1)}, u32[]{:S(2)}, u32[]{:S(2)}) collective-permute-start(f32[2,4,32,384]{3,2,1,0:T(8,128)S(1)} %copy.51), channel_id=1, source_target_pairs={{0,64},{64,128},{128,192},{1,65},{65,129},{129,193},{2,66},{66,130... | collective-permute-start | bytes 1179656 | tf_op jit(solution)/shard_map/ppermute | solution.py:11
  35.8 12.1 %collective-permute-start.1 = (f32[4,1,32,384]{3,2,1,0:T(8,128)}, f32[4,1,32,384]{3,2,1,0:T(8,128)S(1)}, u32[]{:S(2)}, u32[]{:S(2)}) collective-permute-start(f32[4,1,32,384]{3,2,1,0:T(8,128)} %get-tuple-element.71), channel_id=1, source_target_pairs={{0,8},{8,16},{16,24},{24,32},{32,40},{40,48},{48,56},{1,9},{9,17},... | collective-permute-start | bytes 589832 | tf_op jit(solution)/shard_map/ppermute | solution.py:22
  39.4 8.6 %collective-permute-start.2 = (f32[4,1,32,384]{3,2,1,0:T(8,128)}, f32[4,1,32,384]{3,2,1,0:T(8,128)}, u32[]{:S(2)}, u32[]{:S(2)}) collective-permute-start(f32[4,1,32,384]{3,2,1,0:T(8,128)} %get-tuple-element.72), channel_id=1, source_target_pairs={{8,0},{16,8},{24,16},{32,24},{40,32},{48,40},{56,48},{9,1},{17,9},... | collective-permute-start | bytes 589832 | tf_op jit(solution)/shard_map/ppermute | solution.py:24
  50.0 1.5 copy-start.7
  52.1 3.3 %copy-start.1 = (f32[48,3456]{1,0:T(8,128)S(1)}, f32[48,3456]{1,0:T(8,128)}, u32[]{:S(2)}) copy-start(f32[48,3456]{1,0:T(8,128)} %reshape_squeeze.18) | copy-start | bytes 1990660
  52.2 6.3 %copy-start.3 = (f32[48,3456]{1,0:T(8,128)S(1)}, f32[48,3456]{1,0:T(8,128)}, u32[]{:S(2)}) copy-start(f32[48,3456]{1,0:T(8,128)} %reshape_squeeze.20) | copy-start | bytes 1990660
  58.6 9.2 %copy-start.14 = (f32[384]{0:T(512)S(1)}, f32[384]{0:T(512)}, u32[]{:S(2)}) copy-start(f32[384]{0:T(512)} %param.16) | copy-start | bytes 4612
  58.6 15.7 %copy-start.18 = (f32[384]{0:T(512)S(1)}, f32[384]{0:T(512)}, u32[]{:S(2)}) copy-start(f32[384]{0:T(512)} %param.17) | copy-start | bytes 4612
  62.7 9.8 %all-to-all-start = ((f32[8,1,1536]{2,1,0:T(1,128)}), f32[8,1,1536]{2,1,0:T(1,128)S(1)}, u32[]{:S(2)}, u32[]{:S(2)}) async-start(f32[8,1,1536]{2,1,0:T(1,128)} %reshape.280), calls=%async_computation | async-start | bytes 98304 | tf_op jit(solution)/shard_map/all_to_all | solution.py:70
  67.7 157.4 %all-gather.3.cloned.1.call-start = ((), (), s32[]{:S(2)}) async-start(), calls=%async_computation.2 | async-start | bytes 3194880 | tf_op jit(solution)/shard_map/all_gather | solution.py:124
  88.1 17.6 %copy-start.8 = (f32[2,4,32,384]{3,2,1,0:T(8,128)}, f32[2,4,32,384]{3,2,1,0:T(8,128)S(1)}, u32[]{:S(2)}) copy-start(f32[2,4,32,384]{3,2,1,0:T(8,128)S(1)} %copy.62) | copy-start | bytes 1179652
  88.1 12.5 %collective-permute-start.3 = (f32[2,4,32,384]{3,2,1,0:T(8,128)S(1)}, f32[2,4,32,384]{3,2,1,0:T(8,128)S(1)}, u32[]{:S(2)}, u32[]{:S(2)}) collective-permute-start(f32[2,4,32,384]{3,2,1,0:T(8,128)S(1)} %copy.62), channel_id=1, source_target_pairs={{0,64},{64,128},{128,192},{1,65},{65,129},{129,193},{2,66},{66,130... | collective-permute-start | bytes 1179656 | tf_op jit(solution)/shard_map/ppermute | solution.py:11
  101.4 14.3 %collective-permute-start.4 = (f32[4,1,32,384]{3,2,1,0:T(8,128)}, f32[4,1,32,384]{3,2,1,0:T(8,128)S(1)}, u32[]{:S(2)}, u32[]{:S(2)}) collective-permute-start(f32[4,1,32,384]{3,2,1,0:T(8,128)} %get-tuple-element.65), channel_id=1, source_target_pairs={{0,8},{8,16},{16,24},{24,32},{32,40},{40,48},{48,56},{1,9},{9,17},... | collective-permute-start | bytes 589832 | tf_op jit(solution)/shard_map/ppermute | solution.py:22
  105.7 10.0 %collective-permute-start.5 = (f32[4,1,32,384]{3,2,1,0:T(8,128)}, f32[4,1,32,384]{3,2,1,0:T(8,128)}, u32[]{:S(2)}, u32[]{:S(2)}) collective-permute-start(f32[4,1,32,384]{3,2,1,0:T(8,128)} %get-tuple-element.66), channel_id=1, source_target_pairs={{8,0},{16,8},{24,16},{32,24},{40,32},{48,40},{56,48},{9,1},{17,9},... | collective-permute-start | bytes 589832 | tf_op jit(solution)/shard_map/ppermute | solution.py:24
  117.8 1.5 copy-start.9
  119.9 3.3 %copy-start.2 = (f32[48,3456]{1,0:T(8,128)S(1)}, f32[48,3456]{1,0:T(8,128)}, u32[]{:S(2)}) copy-start(f32[48,3456]{1,0:T(8,128)} %reshape_squeeze.21) | copy-start | bytes 1990660
  120.1 6.3 %copy-start.4 = (f32[48,3456]{1,0:T(8,128)S(1)}, f32[48,3456]{1,0:T(8,128)}, u32[]{:S(2)}) copy-start(f32[48,3456]{1,0:T(8,128)} %reshape_squeeze.23) | copy-start | bytes 1990660
  126.4 13.3 %copy-start.13 = (f32[2,4,4,384]{3,2,1,0:T(4,128)S(1)}, f32[2,4,4,384]{3,2,1,0:T(4,128)}, u32[]{:S(2)}) copy-start(f32[2,4,4,384]{3,2,1,0:T(4,128)} %param.13) | copy-start | bytes 147460
  126.4 13.3 %copy-start.15 = (f32[384]{0:T(512)S(1)}, f32[384]{0:T(512)}, u32[]{:S(2)}) copy-start(f32[384]{0:T(512)} %param.19) | copy-start | bytes 4612
  126.4 13.4 %copy-start.17 = (f32[384]{0:T(512)S(1)}, f32[384]{0:T(512)}, u32[]{:S(2)}) copy-start(f32[384]{0:T(512)} %param.20) | copy-start | bytes 4612
  126.4 14.6 %copy-start.10 = (f32[384,384]{1,0:T(8,128)S(1)}, f32[384,384]{1,0:T(8,128)}, u32[]{:S(2)}) copy-start(f32[384,384]{1,0:T(8,128)} %param.23) | copy-start | bytes 1769476
  126.4 15.7 %copy-start.11 = (f32[384,384]{1,0:T(8,128)S(1)}, f32[384,384]{1,0:T(8,128)}, u32[]{:S(2)}) copy-start(f32[384,384]{1,0:T(8,128)} %param.21) | copy-start | bytes 1769476
  141.0 162.6 %all-gather.5.cloned.1.call-start = ((), (), s32[]{:S(2)}) async-start(), calls=%async_computation.3 | async-start | bytes 3194880 | tf_op jit(solution)/shard_map/all_gather | solution.py:125
  142.6 164.6 %copy-start.12 = (f32[384,384]{1,0:T(8,128)S(1)}, f32[384,384]{1,0:T(8,128)}, u32[]{:S(2)}) copy-start(f32[384,384]{1,0:T(8,128)} %param.24) | copy-start | bytes 1769476
  142.6 164.5 %copy-start.16 = (f32[384]{0:T(512)S(1)}, f32[384]{0:T(512)}, u32[]{:S(2)}) copy-start(f32[384]{0:T(512)} %param.25) | copy-start | bytes 4612
Sparse Core Ops, SparseCore 0:
  141.1 83.9 all-gather.2
  227.8 75.7 all-gather.4
where the time goes:
time: 316 us; the launch traced here: 315 us
  waiting for transfers between devices  178 us (56%)
  blocking collectives  38.2 us (12%)
  matrix products  29.9 us (9%)
  local copies, waits for them, and re-layouts  23.7 us (8%)
  starting transfers between devices  21.5 us (7%)
  between operations  14.5 us (5%)
  other arithmetic  9.67 us (3%)
    all_gather x1, waiting for transfers between devices, per_device(): lax.all_gather(keys, ('ha', 'wa'), axis=1, tiled=True)  82.5 us
    all_gather x1, waiting for transfers between devices, per_device(): lax.all_gather(values, ('ha', 'wa'), axis=1, tiled=True)  73.7 us
    all_gather x2, blocking collectives, causal_conv(): widened = lax.all_gather(activated, 'wa', axis=2, tiled=True)  29.6 us
    dot_general x6, matrix products, causal_conv(): lax.dot_general(patches, tap_kernel, (((1,), (1,)), ((), ())), precision=...  18.8 us
    ppermute x2, waiting for transfers between devices, from_behind(): return lax.ppermute(shard, axis, pairs)  16.6 us
    slice x8, local copies, waits for them, and re-layouts, causal_conv(): tap_kernel = kernel[:, time_tap].reshape(out_count, 9 * channels)  10.4 us
    all_to_all x1, blocking collectives, causal_conv(): owned = lax.all_to_all(strip, 'wa', split_axis=2, concat_axis=3, tiled=True)  8.61 us
    ppermute x2, starting transfers between devices, padded_2(): lax.ppermute(tail, axis, [(i, (i + 1) % count) for i in range(ends)])  7.81 us
  transfers between devices with their start and end apart: 9, of which 5 were waited for; matrix products, arithmetic and copies ran while one was open for 7% of the time, Pallas kernels for 0%

commit v1 on v0

--- a/solution.py
+++ b/solution.py
@@ -1,8 +1,42 @@
+import functools
 import math
 import jax
 import jax.numpy as jnp
 from jax import lax
 from jax.sharding import PartitionSpec as P
+
+
+def rails_render(sample, axis_k, content):
+    piece_now = sample.shape
+    return jnp.moveaxis(
+        sample.reshape(
+            *piece_now[:axis_k], content, piece_now[axis_k] // content, *piece_now[axis_k + 1 :]
+        ),
+        axis_k,
+        0,
+    )
+
+
+def series_process(message, d0):
+    message = jnp.moveaxis(message, 0, d0)
+    newest = message.shape
+    return message.reshape(*newest[:d0], newest[d0] * newest[d0 + 1], *newest[d0 + 2 :])
+
+
+def fit_the_vectors(z, net_axis, s0, arr):
+    v1 = lax.axis_size(net_axis)
+    even, reached = (v1, lax.axis_index(net_axis))
+    y1 = rails_render(z, s0, even)
+    by_rank = [y1[reached]]
+    for p in range(1, even):
+        opened = y1[(reached + p) % even]
+        clean = lax.ppermute(opened, net_axis, [(at, (at + p) % even) for at in range(even)])
+        by_rank.append(clean)
+    y1 = jnp.stack(by_rank)[(reached - jnp.arange(even)) % even]
+    return series_process(y1, arr)
+
+
+lead_threads_by_axis = functools.partial(fit_the_vectors, net_axis="wa", s0=2, arr=3)
 
 
 def from_behind(shard, axis, by):
@@ -67,7 +101,7 @@
             preferred_element_type=jnp.float32,
         )
     strip = summed.reshape(frames, heights, widths, out_count)
-    owned = lax.all_to_all(strip, "wa", split_axis=2, concat_axis=3, tiled=True)
+    owned = lead_threads_by_axis(strip)
     return owned + bias
 
 

time: 316 us -> 321 us (1.016); the launches traced: 315 us -> 317 us
  starting transfers between devices: 21.5 us -> 35 us
  blocking collectives: 38.2 us -> 29.3 us
  other arithmetic: 9.67 us -> 6.02 us
    ppermute x0 -> x14, starting transfers between devices: none -> 17.9 us  [fit_the_vectors(): lax.ppermute(opened, net_axis, [(at, (at + p) % even) for at in range(eve...]
    all_to_all x1 -> x0, blocking collectives: 8.61 us -> none  [causal_conv(): owned = lax.all_to_all(strip, 'wa', split_axis=2, concat_axis=3, tiled=True)]
    ppermute x0 -> x14, waiting for transfers between devices: none -> 5.46 us  [fit_the_vectors(): lax.ppermute(opened, net_axis, [(at, (at + p) % even) for at in range(eve...]
    ppermute x2, waiting for transfers between devices: 16.6 us -> 11.5 us  [from_behind(): return lax.ppermute(shard, axis, pairs)]
    all_to_all x1 -> x0, starting transfers between devices: 5 us -> none  [causal_conv(): owned = lax.all_to_all(strip, 'wa', split_axis=2, concat_axis=3, tiled=True)]
    all_to_all x1 -> x0, waiting for transfers between devices: 4.7 us -> none  [causal_conv(): owned = lax.all_to_all(strip, 'wa', split_axis=2, concat_axis=3, tiled=True)]
    ppermute x2, waiting for transfers between devices: 0.01 us -> 4.19 us  [padded_2(): lax.ppermute(head, axis, [((i + 1) % count, i) for i in range(ends)])]
  transfers between devices with their start and end apart: 9 -> 22, of which waited for: 5 -> 12; matrix products, arithmetic and copies ran while one was open for 7% -> 6% of each run, Pallas kernels for 0% -> 0%
where the time goes in v1:
time: 321 us; the launch traced here: 317 us
  waiting for transfers between devices  177 us (55%)
  starting transfers between devices  35 us (11%)
  matrix products  29.9 us (9%)
  blocking collectives  29.3 us (9%)
  local copies, waits for them, and re-layouts  24.4 us (8%)
  between operations  14.7 us (5%)
  other arithmetic  6.02 us (2%)
    all_gather x1, waiting for transfers between devices, per_device(): lax.all_gather(keys, ('ha', 'wa'), axis=1, tiled=True)  81 us
    all_gather x1, waiting for transfers between devices, per_device(): lax.all_gather(values, ('ha', 'wa'), axis=1, tiled=True)  73.7 us
    all_gather x2, blocking collectives, causal_conv(): widened = lax.all_gather(activated, 'wa', axis=2, tiled=True)  29.3 us
    dot_general x6, matrix products, causal_conv(): lax.dot_general(patches, tap_kernel, (((1,), (1,)), ((), ())), precision=...  18.8 us
    ppermute x14, starting transfers between devices, fit_the_vectors(): lax.ppermute(opened, net_axis, [(at, (at + p) % even) for at in range(eve...  17.9 us
    ppermute x2, waiting for transfers between devices, from_behind(): return lax.ppermute(shard, axis, pairs)  11.5 us
    slice x8, local copies, waits for them, and re-layouts, causal_conv(): tap_kernel = kernel[:, time_tap].reshape(out_count, 9 * channels)  8.55 us
    ppermute x2, starting transfers between devices, padded_2(): lax.ppermute(tail, axis, [(i, (i + 1) % count) for i in range(ends)])  7.1 us
  transfers between devices with their start and end apart: 22, of which 12 were waited for; matrix products, arithmetic and copies ran while one was open for 6% of the time, Pallas kernels for 0%

profile of v1, /device:TPU:1, one launch (start us, length us, event | category | flops | bytes accessed | tf_op | source)
XLA Modules:
  0.0 316.5 jit_solution(2892412753452799097)
XLA Ops:
  8.4 16.1 %all_gather.12 = f32[2,4,32,384]{3,1,0,2:T(4,128)S(1)} all-gather(f32[2,4,4,384]{3,1,0,2:T(4,128)S(1)} %copy.44), channel_id=1, replica_groups=mesh['ta'=4,'ha'=8,'wa'=8] {'wa'}, dimensions={2}, use_global_device_ids=true | all-gather | bytes 442368 | tf_op jit(solution)/shard_map/all_gather | solution.py:73
  25.3 2.7 collective-permute-start
  28.0 1.6 fusion.20
  32.7 3.2 %collective-permute-done = f32[2,4,32,384]{3,2,1,0:T(8,128)} collective-permute-done((f32[2,4,32,384]{3,2,1,0:T(8,128)}, f32[2,4,32,384]{3,2,1,0:T(8,128)}, u32[]{:S(2)}, u32[]{:S(2)}) %collective-permute-start) | collective-permute-done | bytes 393248 | tf_op jit(solution)/shard_map/ppermute | solution.py:45
  37.0 3.6 %collective-permute-start.1 = (f32[4,1,32,384]{3,2,1,0:T(8,128)S(1)}, f32[4,1,32,384]{3,2,1,0:T(8,128)S(1)}, u32[]{:S(2)}, u32[]{:S(2)}) collective-permute-start(f32[4,1,32,384]{3,2,1,0:T(8,128)S(1)} %get-tuple-element.71), channel_id=1, source_target_pairs={{0,8},{8,16},{16,24},{24,32},{32,40},{40,48},{48,56},{1,9},{9,17},... | collective-permute-start | bytes 589832 | tf_op jit(solution)/shard_map/ppermute | solution.py:56
  40.6 1.8 collective-permute-start.2
  42.4 1.4 collective-permute-done.1
  43.8 4.2 %collective-permute-done.2 = f32[4,1,32,384]{3,2,1,0:T(8,128)S(1)} collective-permute-done((f32[4,1,32,384]{3,2,1,0:T(8,128)S(1)}, f32[4,1,32,384]{3,2,1,0:T(8,128)S(1)}, u32[]{:S(2)}, u32[]{:S(2)}) %collective-permute-start.2) | collective-permute-done | bytes 196640 | tf_op jit(solution)/shard_map/ppermute | solution.py:58
  50.4 3.1 fusion.26
  56.1 3.1 convolution_add_fusion.4
  59.3 3.1 convolution_add_fusion.3
  62.6 2.9 collective-permute-start.3
  65.5 2.8 collective-permute-start.5
  68.8 2.1 collective-permute-start.7
  73.6 1.4 collective-permute-done.9
  76.1 13.2 %all_gather.13 = f32[2,4,32,384]{3,1,0,2:T(4,128)S(1)} all-gather(f32[2,4,4,384]{3,1,0,2:T(4,128)S(1)} %copy.53), channel_id=1, replica_groups=mesh['ta'=4,'ha'=8,'wa'=8] {'wa'}, dimensions={2}, use_global_device_ids=true | all-gather | bytes 442368 | tf_op jit(solution)/shard_map/all_gather | solution.py:73
  89.4 4.1 %collective-permute-start.10 = (f32[2,4,32,384]{3,2,1,0:T(8,128)S(1)}, f32[2,4,32,384]{3,2,1,0:T(8,128)S(1)}, u32[]{:S(2)}, u32[]{:S(2)}) collective-permute-start(f32[2,4,32,384]{3,2,1,0:T(8,128)S(1)} %copy.54), channel_id=1, source_target_pairs={{0,64},{64,128},{128,192},{1,65},{65,129},{129,193},{2,66},{66,130... | collective-permute-start | bytes 1179656 | tf_op jit(solution)/shard_map/ppermute | solution.py:45
  93.5 8.3 %collective-permute-done.10 = f32[2,4,32,384]{3,2,1,0:T(8,128)S(1)} collective-permute-done((f32[2,4,32,384]{3,2,1,0:T(8,128)S(1)}, f32[2,4,32,384]{3,2,1,0:T(8,128)S(1)}, u32[]{:S(2)}, u32[]{:S(2)}) %collective-permute-start.10) | collective-permute-done | bytes 393248 | tf_op jit(solution)/shard_map/ppermute | solution.py:45
  102.7 3.5 %collective-permute-start.11 = (f32[4,1,32,384]{3,2,1,0:T(8,128)}, f32[4,1,32,384]{3,2,1,0:T(8,128)S(1)}, u32[]{:S(2)}, u32[]{:S(2)}) collective-permute-start(f32[4,1,32,384]{3,2,1,0:T(8,128)} %get-tuple-element.65), channel_id=1, source_target_pairs={{0,8},{8,16},{16,24},{24,32},{32,40},{40,48},{48,56},{1,9},{9,17},... | collective-permute-start | bytes 589832 | tf_op jit(solution)/shard_map/ppermute | solution.py:56
  106.3 1.5 collective-permute-start.12
  107.8 2.7 fusion.19
  111.2 1.4 copy.56
  113.8 1.4 copy.59
  120.8 3.1 fusion.27
  123.9 3.1 convolution_add_fusion.2
  127.2 3.1 convolution_add_fusion.1
  132.7 1.8 collective-permute-start.15
  135.7 2.6 collective-permute-start.17
  145.3 81.0 %all-gather.3.cloned.1.call-done = f32[2,1024,384]{2,1,0:T(8,128)} async-done(((f32[2,16,384]{2,1,0:T(8,128)}), f32[2,1024,384]{2,1,0:T(8,128)}) %all-gather.3.cloned.1.call-update) | async-done | bytes 3145744 | tf_op jit(solution)/shard_map/all_gather | solution.py:158
  226.3 4.6 %fusion.25 = (f32[2,16]{1,0:T(2,128)S(1)}, f32[2,16,1024]{2,1,0:T(8,128)S(1)}) fusion(f32[2,16,384]{2,1,0:T(8,128)S(1)} %fusion.5, f32[2,1024,384]{2,1,0:T(8,128)} %all-gather.3.cloned.1.call-done), kind=kOutput, calls=%fused_computation.165 | convolution fusion | flops 151060448 | bytes 3326080 | tf_op jit(solution)/shard_map/fqc,fkc->fqk/dot_general | solution.py:110
  231.1 73.7 %all-gather.5.cloned.1.call-done = f32[2,1024,384]{2,1,0:T(8,128)} async-done(((f32[2,16,384]{2,1,0:T(8,128)}), f32[2,1024,384]{2,1,0:T(8,128)}) %all-gather.5.cloned.1.call-update) | async-done | bytes 3145744 | tf_op jit(solution)/shard_map/all_gather | solution.py:159
  304.8 3.5 %convolution_divide_fusion = f32[2,16,384]{2,1,0:T(8,128)S(1)} fusion(f32[2,1024,384]{2,1,0:T(8,128)} %all-gather.5.cloned.1.call-done, f32[2,16,1024]{2,1,0:T(8,128)S(1)} %get-tuple-element.88, f32[2,16]{1,0:T(2,128)S(1)} %broadcast_maximum_fusion, f32[2,16]{1,0:T(2,128)S(1)} %fusion.15), kind=kOutput, calls=%fused_computation.19 | convolution fusion | flops 151040000 | bytes 3326208 | tf_op jit(solution)/shard_map/fqk,fkc->fqc/dot_general | solution.py:114
  (185 shorter events, 35.9 us)
Async XLA Ops:
  6.5 136.1 %copy-start = (f32[384,384]{1,0:T(8,128)S(1)}, f32[384,384]{1,0:T(8,128)}, u32[]{:S(2)}) copy-start(f32[384,384]{1,0:T(8,128)} %param.22) | copy-start | bytes 1769476
  6.5 219.8 %all-gather.3.cloned.1.call-start = ((), (), s32[]{:S(2)}) async-start(), calls=%async_computation | async-start | bytes 3194880 | tf_op jit(solution)/shard_map/all_gather | solution.py:158
  25.3 10.6 %collective-permute-start = (f32[2,4,32,384]{3,2,1,0:T(8,128)}, f32[2,4,32,384]{3,2,1,0:T(8,128)}, u32[]{:S(2)}, u32[]{:S(2)}) collective-permute-start(f32[2,4,32,384]{3,2,1,0:T(8,128)} %copy.45), channel_id=1, source_target_pairs={{0,64},{64,128},{128,192},{1,65},{65,129},{129,193},{2,66},{66,130... | collective-permute-start | bytes 1179656 | tf_op jit(solution)/shard_map/ppermute | solution.py:45
  37.0 6.8 %collective-permute-start.1 = (f32[4,1,32,384]{3,2,1,0:T(8,128)S(1)}, f32[4,1,32,384]{3,2,1,0:T(8,128)S(1)}, u32[]{:S(2)}, u32[]{:S(2)}) collective-permute-start(f32[4,1,32,384]{3,2,1,0:T(8,128)S(1)} %get-tuple-element.71), channel_id=1, source_target_pairs={{0,8},{8,16},{16,24},{24,32},{32,40},{40,48},{48,56},{1,9},{9,17},... | collective-permute-start | bytes 589832 | tf_op jit(solution)/shard_map/ppermute | solution.py:56
  40.6 7.4 %collective-permute-start.2 = (f32[4,1,32,384]{3,2,1,0:T(8,128)S(1)}, f32[4,1,32,384]{3,2,1,0:T(8,128)S(1)}, u32[]{:S(2)}, u32[]{:S(2)}) collective-permute-start(f32[4,1,32,384]{3,2,1,0:T(8,128)S(1)} %get-tuple-element.72), channel_id=1, source_target_pairs={{8,0},{16,8},{24,16},{32,24},{40,32},{48,40},{56,48},{9,1},{17,9},... | collective-permute-start | bytes 589832 | tf_op jit(solution)/shard_map/ppermute | solution.py:58
  59.3 16.7 %copy-start.14 = (f32[384]{0:T(512)S(1)}, f32[384]{0:T(512)}, u32[]{:S(2)}) copy-start(f32[384]{0:T(512)} %param.17) | copy-start | bytes 4612
  62.6 8.4 %collective-permute-start.3 = (f32[2,4,4,48]{3,2,1,0:T(4,128)S(1)}, f32[2,4,4,48]{3,2,1,0:T(4,128)S(1)}, u32[]{:S(2)}, u32[]{:S(2)}) collective-permute-start(f32[2,4,4,48]{3,2,1,0:T(4,128)S(1)} %get-tuple-element.86), channel_id=1, source_target_pairs={{0,1},{1,2},{2,3},{3,4},{4,5},{5,6},{6,7},{7,0},{8,9},{9,10},{10,1... | collective-permute-start | bytes 18440 | tf_op jit(solution)/shard_map/ppermute | solution.py:33
  65.5 5.9 %collective-permute-start.4 = (f32[2,4,4,48]{3,2,1,0:T(4,128)S(1)}, f32[2,4,4,48]{3,2,1,0:T(4,128)S(1)}, u32[]{:S(2)}, u32[]{:S(2)}) collective-permute-start(f32[2,4,4,48]{3,2,1,0:T(4,128)S(1)} %get-tuple-element.85), channel_id=1, source_target_pairs={{0,2},{1,3},{2,4},{3,5},{4,6},{5,7},{6,0},{7,1},{8,10},{9,11},{10,... | collective-permute-start | bytes 18440 | tf_op jit(solution)/shard_map/ppermute | solution.py:33
  65.5 6.3 %collective-permute-start.5 = (f32[2,4,4,48]{3,2,1,0:T(4,128)S(1)}, f32[2,4,4,48]{3,2,1,0:T(4,128)S(1)}, u32[]{:S(2)}, u32[]{:S(2)}) collective-permute-start(f32[2,4,4,48]{3,2,1,0:T(4,128)S(1)} %get-tuple-element.84), channel_id=1, source_target_pairs={{0,3},{1,4},{2,5},{3,6},{4,7},{5,0},{6,1},{7,2},{8,11},{9,12},{10,... | collective-permute-start | bytes 18440 | tf_op jit(solution)/shard_map/ppermute | solution.py:33
  68.2 4.4 %collective-permute-start.6 = (f32[2,4,4,48]{3,2,1,0:T(4,128)S(1)}, f32[2,4,4,48]{3,2,1,0:T(4,128)S(1)}, u32[]{:S(2)}, u32[]{:S(2)}) collective-permute-start(f32[2,4,4,48]{3,2,1,0:T(4,128)S(1)} %get-tuple-element.83), channel_id=1, source_target_pairs={{0,4},{1,5},{2,6},{3,7},{4,0},{5,1},{6,2},{7,3},{8,12},{9,13},{10,... | collective-permute-start | bytes 18440 | tf_op jit(solution)/shard_map/ppermute | solution.py:33
  68.8 4.7 %collective-permute-start.7 = (f32[2,4,4,48]{3,2,1,0:T(4,128)S(1)}, f32[2,4,4,48]{3,2,1,0:T(4,128)S(1)}, u32[]{:S(2)}, u32[]{:S(2)}) collective-permute-start(f32[2,4,4,48]{3,2,1,0:T(4,128)S(1)} %get-tuple-element.82), channel_id=1, source_target_pairs={{0,5},{1,6},{2,7},{3,0},{4,1},{5,2},{6,3},{7,4},{8,13},{9,14},{10,... | collective-permute-start | bytes 18440 | tf_op jit(solution)/shard_map/ppermute | solution.py:33
  71.0 2.6 collective-permute-start.8
  71.4 3.6 %collective-permute-start.9 = (f32[2,4,4,48]{3,2,1,0:T(4,128)S(1)}, f32[2,4,4,48]{3,2,1,0:T(4,128)S(1)}, u32[]{:S(2)}, u32[]{:S(2)}) collective-permute-start(f32[2,4,4,48]{3,2,1,0:T(4,128)S(1)} %get-tuple-element.80), channel_id=1, source_target_pairs={{0,7},{1,0},{2,1},{3,2},{4,3},{5,4},{6,5},{7,6},{8,15},{9,8},{10,9... | collective-permute-start | bytes 18440 | tf_op jit(solution)/shard_map/ppermute | solution.py:33
  89.4 16.9 %copy-start.4 = (f32[2,4,32,384]{3,2,1,0:T(8,128)}, f32[2,4,32,384]{3,2,1,0:T(8,128)S(1)}, u32[]{:S(2)}) copy-start(f32[2,4,32,384]{3,2,1,0:T(8,128)S(1)} %copy.54) | copy-start | bytes 1179652
  89.4 12.5 %collective-permute-start.10 = (f32[2,4,32,384]{3,2,1,0:T(8,128)S(1)}, f32[2,4,32,384]{3,2,1,0:T(8,128)S(1)}, u32[]{:S(2)}, u32[]{:S(2)}) collective-permute-start(f32[2,4,32,384]{3,2,1,0:T(8,128)S(1)} %copy.54), channel_id=1, source_target_pairs={{0,64},{64,128},{128,192},{1,65},{65,129},{129,193},{2,66},{66,130... | collective-permute-start | bytes 1179656 | tf_op jit(solution)/shard_map/ppermute | solution.py:45
  102.7 13.7 %collective-permute-start.11 = (f32[4,1,32,384]{3,2,1,0:T(8,128)}, f32[4,1,32,384]{3,2,1,0:T(8,128)S(1)}, u32[]{:S(2)}, u32[]{:S(2)}) collective-permute-start(f32[4,1,32,384]{3,2,1,0:T(8,128)} %get-tuple-element.65), channel_id=1, source_target_pairs={{0,8},{8,16},{16,24},{24,32},{32,40},{40,48},{48,56},{1,9},{9,17},... | collective-permute-start | bytes 589832 | tf_op jit(solution)/shard_map/ppermute | solution.py:56
  106.3 10.2 %collective-permute-start.12 = (f32[4,1,32,384]{3,2,1,0:T(8,128)}, f32[4,1,32,384]{3,2,1,0:T(8,128)}, u32[]{:S(2)}, u32[]{:S(2)}) collective-permute-start(f32[4,1,32,384]{3,2,1,0:T(8,128)} %get-tuple-element.66), channel_id=1, source_target_pairs={{8,0},{16,8},{24,16},{32,24},{40,32},{48,40},{56,48},{9,1},{17,9},... | collective-permute-start | bytes 589832 | tf_op jit(solution)/shard_map/ppermute | solution.py:58
  127.1 15.3 %copy-start.9 = (f32[2,4,4,384]{3,2,1,0:T(4,128)S(1)}, f32[2,4,4,384]{3,2,1,0:T(4,128)}, u32[]{:S(2)}) copy-start(f32[2,4,4,384]{3,2,1,0:T(4,128)} %param.13) | copy-start | bytes 147460
  127.1 15.3 %copy-start.11 = (f32[384]{0:T(512)S(1)}, f32[384]{0:T(512)}, u32[]{:S(2)}) copy-start(f32[384]{0:T(512)} %param.19) | copy-start | bytes 4612
  127.1 15.4 %copy-start.13 = (f32[384]{0:T(512)S(1)}, f32[384]{0:T(512)}, u32[]{:S(2)}) copy-start(f32[384]{0:T(512)} %param.20) | copy-start | bytes 4612
  127.1 16.6 %copy-start.6 = (f32[384,384]{1,0:T(8,128)S(1)}, f32[384,384]{1,0:T(8,128)}, u32[]{:S(2)}) copy-start(f32[384,384]{1,0:T(8,128)} %param.23) | copy-start | bytes 1769476
  127.2 17.7 %copy-start.7 = (f32[384,384]{1,0:T(8,128)S(1)}, f32[384,384]{1,0:T(8,128)}, u32[]{:S(2)}) copy-start(f32[384,384]{1,0:T(8,128)} %param.21) | copy-start | bytes 1769476
  130.5 7.8 %collective-permute-start.13 = (f32[2,4,4,48]{3,2,1,0:T(4,128)S(1)}, f32[2,4,4,48]{3,2,1,0:T(4,128)S(1)}, u32[]{:S(2)}, u32[]{:S(2)}) collective-permute-start(f32[2,4,4,48]{3,2,1,0:T(4,128)S(1)} %get-tuple-element.79), channel_id=1, source_target_pairs={{0,1},{1,2},{2,3},{3,4},{4,5},{5,6},{6,7},{7,0},{8,9},{9,10},{10,1... | collective-permute-start | bytes 18440 | tf_op jit(solution)/shard_map/ppermute | solution.py:33
  131.5 6.8 %collective-permute-start.14 = (f32[2,4,4,48]{3,2,1,0:T(4,128)S(1)}, f32[2,4,4,48]{3,2,1,0:T(4,128)S(1)}, u32[]{:S(2)}, u32[]{:S(2)}) collective-permute-start(f32[2,4,4,48]{3,2,1,0:T(4,128)S(1)} %get-tuple-element.78), channel_id=1, source_target_pairs={{0,2},{1,3},{2,4},{3,5},{4,6},{5,7},{6,0},{7,1},{8,10},{9,11},{10,... | collective-permute-start | bytes 18440 | tf_op jit(solution)/shard_map/ppermute | solution.py:33
  132.7 6.5 %collective-permute-start.15 = (f32[2,4,4,48]{3,2,1,0:T(4,128)S(1)}, f32[2,4,4,48]{3,2,1,0:T(4,128)S(1)}, u32[]{:S(2)}, u32[]{:S(2)}) collective-permute-start(f32[2,4,4,48]{3,2,1,0:T(4,128)S(1)} %get-tuple-element.77), channel_id=1, source_target_pairs={{0,3},{1,4},{2,5},{3,6},{4,7},{5,0},{6,1},{7,2},{8,11},{9,12},{10,... | collective-permute-start | bytes 18440 | tf_op jit(solution)/shard_map/ppermute | solution.py:33
  134.5 4.7 %collective-permute-start.16 = (f32[2,4,4,48]{3,2,1,0:T(4,128)S(1)}, f32[2,4,4,48]{3,2,1,0:T(4,128)S(1)}, u32[]{:S(2)}, u32[]{:S(2)}) collective-permute-start(f32[2,4,4,48]{3,2,1,0:T(4,128)S(1)} %get-tuple-element.76), channel_id=1, source_target_pairs={{0,4},{1,5},{2,6},{3,7},{4,0},{5,1},{6,2},{7,3},{8,12},{9,13},{10,... | collective-permute-start | bytes 18440 | tf_op jit(solution)/shard_map/ppermute | solution.py:33
  135.7 4.7 %collective-permute-start.17 = (f32[2,4,4,48]{3,2,1,0:T(4,128)S(1)}, f32[2,4,4,48]{3,2,1,0:T(4,128)S(1)}, u32[]{:S(2)}, u32[]{:S(2)}) collective-permute-start(f32[2,4,4,48]{3,2,1,0:T(4,128)S(1)} %get-tuple-element.75), channel_id=1, source_target_pairs={{0,5},{1,6},{2,7},{3,0},{4,1},{5,2},{6,3},{7,4},{8,13},{9,14},{10,... | collective-permute-start | bytes 18440 | tf_op jit(solution)/shard_map/ppermute | solution.py:33
  138.3 3.0 collective-permute-start.18
  138.3 3.2 %collective-permute-start.19 = (f32[2,4,4,48]{3,2,1,0:T(4,128)S(1)}, f32[2,4,4,48]{3,2,1,0:T(4,128)S(1)}, u32[]{:S(2)}, u32[]{:S(2)}) collective-permute-start(f32[2,4,4,48]{3,2,1,0:T(4,128)S(1)} %get-tuple-element.73), channel_id=1, source_target_pairs={{0,7},{1,0},{2,1},{3,2},{4,3},{5,4},{6,5},{7,6},{8,15},{9,8},{10,9... | collective-permute-start | bytes 18440 | tf_op jit(solution)/shard_map/ppermute | solution.py:33
  143.7 161.2 %all-gather.5.cloned.1.call-start = ((), (), s32[]{:S(2)}) async-start(), calls=%async_computation.1 | async-start | bytes 3194880 | tf_op jit(solution)/shard_map/all_gather | solution.py:159
  145.3 163.1 %copy-start.8 = (f32[384,384]{1,0:T(8,128)S(1)}, f32[384,384]{1,0:T(8,128)}, u32[]{:S(2)}) copy-start(f32[384,384]{1,0:T(8,128)} %param.24) | copy-start | bytes 1769476
  145.3 163.1 %copy-start.12 = (f32[384]{0:T(512)S(1)}, f32[384]{0:T(512)}, u32[]{:S(2)}) copy-start(f32[384]{0:T(512)} %param.25) | copy-start | bytes 4612
  (5 other events, 14.9 us)
Sparse Core Ops, SparseCore 0:
  143.8 82.4 all-gather.2
  229.0 75.7 all-gather.4
